TPU v7x, 512 devices: a whole 4x8x8 slice. The times are simulated.
512 devices in a mesh: tp: 8 (over z), ad: 64 (over y, x, core).
Axes of the slice: x: 4, y: 8, z: 8, core: 2. Of those that a mesh axis runs over, the one named last changes fastest.
Arguments:
- tokens: bfloat16 [65536, 8192], P('ad', 'tp'), may hold values from -6 to 6
- value_weight: bfloat16 [8192, 1024], P(('tp', 'ad')), may hold values from -0.0625 to 0.0625
- adapter_down: bfloat16 [128, 8192, 128], P('ad', 'tp'), may hold values from -0.0625 to 0.0625
- adapter_up_panels: bfloat16 [128, 128, 1024], P('ad', None, 'tp'), may hold values from -0.5 to 0.5
- req_start: int32 [64], replicated, may hold values from 0 to 65280, as said below
- req_adapter: int32 [64], replicated, may hold values from 0 to 127
- adapter_home: int32 [128], replicated, may hold values from 0 to 127, each once
Outputs:
- adapted: bfloat16 [65536, 1024], P('ad', 'tp')
Inputs may be any that keep to these rules, and one draw needn't show every extreme that they name: `req_start`: entries rise strictly, the first is 0 and each is a multiple of 256; the tokens of one index of ad meet at most 4 requests, and those of the first index meet exactly 4. Each storage row once; adapter a is stored on index adapter_home[a] // 2 of ad.
All inputs are finite; a program needn't handle non-finite values.
Results may differ from a plain program's by a relative error of at most 0.0085.
Values may be sent and summed in bfloat16 or wider, within the bound.
A program may use at most 64 MiB of HBM per device.

v0:
```python
import jax
import jax.numpy as jnp
from jax import lax
from jax.sharding import PartitionSpec as P

FMAX = 4


adapter_scale = 2.0


def body(
    tokens, value_weight, adapter_down, adapter_up_panels, req_start, req_adapter, adapter_home
):
    tok_rows = tokens.shape[0]
    width_shard = tokens.shape[1]
    ad_count = lax.axis_size("ad")
    slot_count = FMAX
    block_rows = tok_rows // slot_count
    owned_count = adapter_down.shape[0]
    rank_width = adapter_down.shape[2]
    out_cols = adapter_up_panels.shape[2]
    slab_rows = width_shard // ad_count
    rank_slab = rank_width // ad_count
    total_adapters = owned_count * ad_count
    base_part = jnp.dot(
        tokens,
        lax.all_gather(value_weight, "ad", axis=0, tiled=True),
        preferred_element_type=jnp.float32,
    )
    down_send = adapter_down.reshape(owned_count, ad_count, slab_rows, rank_width)
    up_send = adapter_up_panels.reshape(owned_count, ad_count, rank_slab, out_cols)
    down_slab, up_slab = (
        lax.all_to_all(down_send, "ad", split_axis=1, concat_axis=0, tiled=True),
        lax.all_to_all(up_send, "ad", split_axis=1, concat_axis=0, tiled=True),
    )
    down_slab = down_slab.reshape(total_adapters, slab_rows, rank_width)
    up_slab = up_slab.reshape(total_adapters, rank_slab, out_cols)
    requests = req_start.shape[0]
    req_ids = jnp.arange(requests, dtype=jnp.int32)
    first_rows = jnp.arange(ad_count, dtype=jnp.int32) * tok_rows
    first_req = jnp.sum((req_start[None, :] <= first_rows[:, None]).astype(jnp.int32), axis=1) - 1
    wanted = jnp.minimum(
        first_req[:, None] + jnp.arange(slot_count, dtype=jnp.int32)[None, :], requests - 1
    )
    chosen = jnp.sum(
        jnp.where(wanted[:, :, None] == req_ids[None, None, :], req_adapter[None, None, :], 0),
        axis=2,
    )
    adapter_ids = jnp.arange(total_adapters, dtype=jnp.int32)
    storage = jnp.sum(
        jnp.where(chosen[:, :, None] == adapter_ids[None, None, :], adapter_home[None, None, :], 0),
        axis=2,
    )
    fetch_rows = storage.T
    down_out = jnp.take(down_slab, fetch_rows, axis=0)
    up_out = jnp.take(up_slab, fetch_rows, axis=0)
    down_got, up_got = (
        lax.all_to_all(down_out, "ad", split_axis=1, concat_axis=1, tiled=True),
        lax.all_to_all(up_out, "ad", split_axis=1, concat_axis=1, tiled=True),
    )
    down_got = down_got.reshape(slot_count, width_shard, rank_width)
    up_got = up_got.reshape(slot_count, rank_width, out_cols)
    my_index = lax.axis_index("ad")
    block_first = my_index * tok_rows + jnp.arange(slot_count, dtype=jnp.int32) * block_rows
    block_req = jnp.sum((req_start[None, :] <= block_first[:, None]).astype(jnp.int32), axis=1) - 1
    mine_first = jnp.sum((req_start <= my_index * tok_rows).astype(jnp.int32)) - 1
    block_slot = block_req - mine_first
    block_down = jnp.take(down_got, block_slot, axis=0)
    block_up = jnp.take(up_got, block_slot, axis=0)
    tok_blocks = tokens.reshape(slot_count, block_rows, width_shard)
    rank_part = jnp.einsum(
        "btd,bdr->btr", tok_blocks, block_down, preferred_element_type=jnp.float32
    ).reshape(tok_rows, rank_width)
    rank_full = lax.psum(rank_part, "tp")
    base_value_share = lax.psum_scatter(
        base_part.astype(jnp.bfloat16), "tp", scatter_dimension=1, tiled=True
    ).astype(jnp.float32)
    rank_rounded = rank_full.astype(jnp.bfloat16)
    rank_blocks = rank_rounded.reshape(slot_count, block_rows, rank_width)
    adapter_value_delta = jnp.einsum(
        "btr,brk->btk", rank_blocks, block_up, preferred_element_type=jnp.float32
    ).reshape(tok_rows, out_cols)
    return (base_value_share + adapter_scale * adapter_value_delta).astype(jnp.bfloat16)


def solution(mesh):
    return jax.shard_map(
        body,
        mesh=mesh,
        in_specs=(
            P("ad", "tp"),
            P(("tp", "ad"), None),
            P("ad", "tp", None),
            P("ad", None, "tp"),
            P(),
            P(),
            P(),
        ),
        out_specs=P("ad", "tp"),
        check_vma=False,
    )
```

profile of v0, /device:TPU:6, one launch (start us, length us, event | category | flops | bytes accessed | tf_op | source)
XLA Modules:
  0.0 214.8 jit_solution(15001548889522600527)
XLA Ops:
  6.5 0.0 copy-start
  6.5 0.0 all-gather.2.cloned.1.call-start
  6.5 0.7 all-gather.2.cloned.1.call-update
  7.3 1.5 copy.37
  8.8 10.6 %all-to-all-start.2 = ((bf16[2,64,2,128]{3,0,2,1:T(2,128)(2,1)}), bf16[2,64,2,128]{3,0,2,1:T(2,128)(2,1)S(1)}, u32[]{:S(2)}, u32[]{:S(2)}) async-start(bf16[2,64,2,128]{3,0,2,1:T(2,128)(2,1)} %bitcast.13), calls=%async_computation.2 | async-start | bytes 131072 | tf_op jit(solution)/shard_map/all_to_all | solution.py:35
  19.4 0.8 convert_reduce_fusion
  20.3 0.9 select_reduce_fusion.1
  21.2 1.9 copy.31
  23.0 0.9 select_reduce_fusion
  23.9 3.5 %all-to-all-done.2 = bf16[2,64,2,128]{3,0,2,1:T(2,128)(2,1)S(1)} async-done(((bf16[2,64,2,128]{3,0,2,1:T(2,128)(2,1)}), bf16[2,64,2,128]{3,0,2,1:T(2,128)(2,1)S(1)}, u32[]{:S(2)}, u32[]{:S(2)}) %all-to-all-start.2) | async-done | bytes 65568 | tf_op jit(solution)/shard_map/all_to_all | solution.py:35
  27.4 6.8 %all-to-all-start = ((bf16[2,64,16,128]{3,2,0,1:T(8,128)(2,1)}), bf16[2,64,16,128]{3,2,0,1:T(8,128)(2,1)S(1)}, u32[]{:S(2)}, u32[]{:S(2)}) async-start(bf16[2,64,16,128]{3,2,0,1:T(8,128)(2,1)} %copy.31), calls=%async_computation | async-start | bytes 1048576 | tf_op jit(solution)/shard_map/all_to_all | solution.py:34
  34.2 0.0 reduce-scatter.4.cloned.1.call-start
  34.3 63.4 %all-gather.2.cloned.1.call-done = bf16[1024,1024]{1,0:T(8,128)(2,1)} async-done(((bf16[16,1024]{1,0:T(8,128)(2,1)}), bf16[1024,1024]{1,0:T(8,128)(2,1)}) %all-gather.2.cloned.1.call-update) | async-done | bytes 2097168 | tf_op jit(solution)/shard_map/all_gather | solution.py:28
  97.7 0.0 copy-done
  97.7 5.2 %convolution_convert_fusion = bf16[1024,1024]{1,0:T(8,128)(2,1)} fusion(bf16[1024,1024]{1,0:T(8,128)(2,1)S(1)} %copy-done, bf16[1024,1024]{1,0:T(8,128)(2,1)} %all-gather.2.cloned.1.call-done), kind=kOutput, calls=%fused_computation.4 | convolution fusion | flops 2148532224 | bytes 6291456 | tf_op jit(solution)/shard_map/dot_general | solution.py:26
  102.9 4.0 %copy.43 = bf16[1024,1024]{0,1:T(8,128)(2,1)} copy(bf16[1024,1024]{1,0:T(8,128)(2,1)} %convolution_convert_fusion) | data formatting | bytes 4194304
  106.9 0.0 reduce-scatter.4.cloned.1.call-update
  106.9 0.1 reshape.113
  107.0 0.1 copy.30
  107.2 0.1 copy.39
  107.3 0.9 gather_fusion.2
  108.2 1.0 broadcast_select_fusion
  109.2 0.0 all-to-all-done
  109.2 8.0 %all-to-all-start.3 = ((bf16[4,64,2,128]{3,2,0,1:T(2,128)(2,1)}), bf16[4,64,2,128]{3,2,0,1:T(2,128)(2,1)S(1)}, u32[]{:S(2)}, u32[]{:S(2)}) async-start(bf16[4,64,2,128]{3,2,0,1:T(2,128)(2,1)} %broadcast_select_fusion), calls=%async_computation.3 | async-start | bytes 262144 | tf_op jit(solution)/shard_map/all_to_all | solution.py:60
  117.2 1.8 gather_fusion
  118.9 0.0 copy-start.1
  118.9 2.3 %copy_select_fusion = bf16[4,64,16,128]{3,2,0,1:T(8,128)(2,1)} fusion(bf16[4,64,16,128]{3,2,1,0:T(8,128)(2,1)} %bitcast.41, pred[4,64]{0,1:T(8,128)(4,1)S(1)} %copy.30), kind=kLoop, calls=%fused_computation.7 | loop fusion | flops 524288 | bytes 2097408 | tf_op jit(solution)/shard_map/jit(_take)/select_n | solution.py:56
  121.2 5.1 %all-to-all-done.3 = bf16[4,64,2,128]{3,2,0,1:T(2,128)(2,1)S(1)} async-done(((bf16[4,64,2,128]{3,2,0,1:T(2,128)(2,1)}), bf16[4,64,2,128]{3,2,0,1:T(2,128)(2,1)S(1)}, u32[]{:S(2)}, u32[]{:S(2)}) %all-to-all-start.3) | async-done | bytes 131104 | tf_op jit(solution)/shard_map/all_to_all | solution.py:60
  126.3 7.3 %all-to-all-start.1 = ((bf16[4,64,16,128]{3,2,0,1:T(8,128)(2,1)}), bf16[4,64,16,128]{3,2,0,1:T(8,128)(2,1)}, u32[]{:S(2)}, u32[]{:S(2)}) async-start(bf16[4,64,16,128]{3,2,0,1:T(8,128)(2,1)} %copy_select_fusion), calls=%async_computation.1 | async-start | bytes 2097152 | tf_op jit(solution)/shard_map/all_to_all | solution.py:59
  133.6 0.0 copy-done.1
  133.6 0.6 fusion.7
  134.9 0.2 convert_reduce_fusion.1
  135.1 0.1 copy.41
  135.2 0.6 gather_fusion.3
  135.8 26.6 %all-to-all-done.1 = bf16[4,64,16,128]{3,2,0,1:T(8,128)(2,1)} async-done(((bf16[4,64,16,128]{3,2,0,1:T(8,128)(2,1)}), bf16[4,64,16,128]{3,2,0,1:T(8,128)(2,1)}, u32[]{:S(2)}, u32[]{:S(2)}) %all-to-all-start.1) | async-done | bytes 1048608 | tf_op jit(solution)/shard_map/all_to_all | solution.py:59
  162.4 1.4 copy.33
  163.8 1.7 gather_fusion.1
  165.5 2.1 convolution_bitcast_fusion
  167.6 0.2 copy.35
  167.8 38.0 %all-reduce.1 = bf16[1024,128]{1,0:T(8,128)(2,1)S(1)} all-reduce(f32[1024,128]{1,0:T(8,128)S(1)} %bitcast.43), channel_id=1, replica_groups=mesh['tp'=8,'ad'=64] {'tp'}, use_global_device_ids=true, to_apply=%region_6.7 | all-reduce | flops 131072 | bytes 786432 | tf_op jit(solution)/shard_map/psum | solution.py:75
  205.8 0.3 convolution_multiply_fusion
  206.1 0.0 reduce-scatter.4.cloned.1.call-done
  206.1 1.1 copy.44
  207.2 0.8 fusion.2
  (11 shorter events, 0.1 us)
Async XLA Ops:
  6.5 91.2 %copy-start = (bf16[1024,1024]{1,0:T(8,128)(2,1)S(1)}, bf16[1024,1024]{1,0:T(8,128)(2,1)}, u32[]{:S(2)}) copy-start(bf16[1024,1024]{1,0:T(8,128)(2,1)} %param.7) | copy-start | bytes 6291460
  6.5 91.2 %all-gather.2.cloned.1.call-start = ((), (), s32[]{:S(2)}) async-start(), calls=%async_computation.5 | async-start | bytes 2129920 | tf_op jit(solution)/shard_map/all_gather | solution.py:28
  8.8 18.6 %all-to-all-start.2 = ((bf16[2,64,2,128]{3,0,2,1:T(2,128)(2,1)}), bf16[2,64,2,128]{3,0,2,1:T(2,128)(2,1)S(1)}, u32[]{:S(2)}, u32[]{:S(2)}) async-start(bf16[2,64,2,128]{3,0,2,1:T(2,128)(2,1)} %bitcast.13), calls=%async_computation.2 | async-start | bytes 131072 | tf_op jit(solution)/shard_map/all_to_all | solution.py:35
  27.4 81.8 %all-to-all-start = ((bf16[2,64,16,128]{3,2,0,1:T(8,128)(2,1)}), bf16[2,64,16,128]{3,2,0,1:T(8,128)(2,1)S(1)}, u32[]{:S(2)}, u32[]{:S(2)}) async-start(bf16[2,64,16,128]{3,2,0,1:T(8,128)(2,1)} %copy.31), calls=%async_computation | async-start | bytes 1048576 | tf_op jit(solution)/shard_map/all_to_all | solution.py:34
  34.2 171.8 %reduce-scatter.4.cloned.1.call-start = ((), (), s32[]{:S(2)}) async-start(), calls=%async_computation.6 | async-start | bytes 2359296
  109.2 17.1 %all-to-all-start.3 = ((bf16[4,64,2,128]{3,2,0,1:T(2,128)(2,1)}), bf16[4,64,2,128]{3,2,0,1:T(2,128)(2,1)S(1)}, u32[]{:S(2)}, u32[]{:S(2)}) async-start(bf16[4,64,2,128]{3,2,0,1:T(2,128)(2,1)} %broadcast_select_fusion), calls=%async_computation.3 | async-start | bytes 262144 | tf_op jit(solution)/shard_map/all_to_all | solution.py:60
  118.9 14.7 %copy-start.1 = (s32[64]{0:T(128)S(1)}, s32[64]{0:T(128)}, u32[]{:S(2)}) copy-start(s32[64]{0:T(128)} %param.11) | copy-start | bytes 772
  126.3 36.1 %all-to-all-start.1 = ((bf16[4,64,16,128]{3,2,0,1:T(8,128)(2,1)}), bf16[4,64,16,128]{3,2,0,1:T(8,128)(2,1)}, u32[]{:S(2)}, u32[]{:S(2)}) async-start(bf16[4,64,16,128]{3,2,0,1:T(8,128)(2,1)} %copy_select_fusion), calls=%async_computation.1 | async-start | bytes 2097152 | tf_op jit(solution)/shard_map/all_to_all | solution.py:59
Sparse Core Ops, SparseCore 0:
  10.7 86.9 all-gather.1
  107.0 44.5 reduce-scatter.3
where the time goes:
time: 216 us; the launch traced here: 215 us
  waiting for transfers between devices  99.4 us (46%)
  blocking collectives  38 us (18%)
  starting transfers between devices  32.6 us (15%)
  local copies, waits for them, and re-layouts  15.4 us (7%)
  between operations  14.2 us (7%)
  matrix products  7.62 us (4%)
  other arithmetic  7.53 us (3%)
    all_gather x1, waiting for transfers between devices, body(): lax.all_gather(value_weight, 'ad', axis=0, tiled=True)  63.4 us
    psum x1, blocking collectives, body(): rank_full = lax.psum(rank_part, 'tp')  38 us
    all_to_all x1, waiting for transfers between devices, body(): lax.all_to_all(down_out, 'ad', split_axis=1, concat_axis=1, tiled=True)  26.6 us
    all_to_all x1, starting transfers between devices, body(): lax.all_to_all(up_send, 'ad', split_axis=1, concat_axis=0, tiled=True)  10.6 us
    all_to_all x1, starting transfers between devices, body(): lax.all_to_all(up_out, 'ad', split_axis=1, concat_axis=1, tiled=True)  7.96 us
    all_to_all x1, starting transfers between devices, body(): lax.all_to_all(down_out, 'ad', split_axis=1, concat_axis=1, tiled=True)  7.26 us
    all_to_all x1, starting transfers between devices, body(): lax.all_to_all(down_send, 'ad', split_axis=1, concat_axis=0, tiled=True)  6.79 us
    unnamed x7, local copies, waits for them, and re-layouts  6.62 us
  transfers between devices with their start and end apart: 6, of which 4 were waited for; matrix products, arithmetic and copies ran while one was open for 13% of the time, Pallas kernels for 0%

commit v1 on v0

v1 whole, which is shorter than its diff:
```python
import functools

import jax
import jax.numpy as jnp
from jax import lax
from jax.experimental import pallas as pl
from jax.experimental.pallas import tpu as pltpu
from jax.sharding import PartitionSpec as P

BF = jnp.bfloat16
F32 = jnp.float32
MESH = pl.DeviceIdType.MESH

ROW = 8
NX = 4
NT = 8
NY = 8
BLK = 4
SPREAD = (1, 7, 2, 6, 3, 5, 4)
PIECES = (4, 3, 5, 2, 6, 1, 7, 0)
ADAPTER_SCALE = 2.0


def kernel(
    tok_h, vw_h, down_h, up_h, start_s, adap_s, home_s,
    out_ref,
    tok, wy, wb, dnrow, slab, dsel, drow, dfin,
    uprow, uperm, upslab, upsel, uprcv, upx, upg,
    zs, zr, part, rsend, rrecv, rfull, ids,
    loc_sem, w1s, w1r, w2s, w2r, w3s, w3r,
    a1s, a1r, u1s, u1r, b1s, b1r, v1s, v1r,
    a2s, a2r, u2s, u2r, b2s, b2r, v2s, v2r,
    zss, zrs, rss, rsr, rgs, rgr,
):
    t = lax.axis_index("tp")
    a = lax.axis_index("ad")
    y = a // ROW
    q = a % ROW
    x = q // 2
    c = q % 2

    def ydev(d):
        return (t, ((y + d) % NY) * ROW + q)

    def rdev(e):
        return (t, y * ROW + (q + e) % ROW)

    def xdev(f):
        return (t, y * ROW + ((x + f) % NX) * 2 + c)

    def tdev(k):
        return ((t + k) % NT, a)

    sib = (t, y * ROW + x * 2 + (1 - c))

    bar = pltpu.get_barrier_semaphore()
    for d in range(1, NY):
        pl.semaphore_signal(bar, inc=1, device_id=ydev(d), device_id_type=MESH)
    for e in range(1, ROW):
        pl.semaphore_signal(bar, inc=1, device_id=rdev(e), device_id_type=MESH)
    for k in range(1, NT):
        pl.semaphore_signal(bar, inc=1, device_id=tdev(k), device_id_type=MESH)
    pl.semaphore_wait(bar, 21)

    sent = []

    def remote(src, dst, s, r, dev):
        cp = pltpu.make_async_remote_copy(
            src_ref=src, dst_ref=dst, send_sem=s, recv_sem=r, device_id=dev, device_id_type=MESH
        )
        cp.start()
        sent.append(cp)
        return cp

    def local(src, dst, i):
        cp = pltpu.make_async_copy(src, dst, loc_sem.at[i])
        cp.start()
        return cp

    a1 = [
        remote(down_h.at[:, (q + e) % ROW], dnrow.at[pl.ds(2 * q, 2)], a1s.at[e], a1r.at[e], rdev(e))
        for e in SPREAD
    ]
    cd = local(down_h.at[:, q], dnrow.at[pl.ds(2 * q, 2)], 1)
    w1 = [remote(vw_h, wy.at[y], w1s.at[d], w1r.at[d], ydev(d)) for d in SPREAD]
    cw = local(vw_h, wy.at[y], 0)
    u1 = [
        remote(up_h.at[:, (q + e) % ROW], uprow.at[pl.ds(2 * q, 2)], u1s.at[e], u1r.at[e], rdev(e))
        for e in SPREAD
    ]
    cu = local(up_h.at[:, q], uprow.at[pl.ds(2 * q, 2)], 2)
    ct = local(tok_h, tok, 3)

    cd.wait()
    for cp in a1:
        cp.wait_recv()
    b1 = [
        remote(dnrow.at[:, (y + d) % NY], slab.at[pl.ds(16 * y, 16)], b1s.at[d], b1r.at[d], ydev(d))
        for d in SPREAD
    ]
    cs = local(dnrow.at[:, y], slab.at[pl.ds(16 * y, 16)], 4)
    def cols(o):
        return pl.ds(pl.multiple_of(((t + o) % NT) * 128, 128), 128)

    cw.wait()
    for cp in w1:
        cp.wait_recv()
    w2 = []
    for p, o in enumerate(PIECES):
        w2.append([
            remote(
                wy.at[:, :, cols(o)], wb[p].at[c, x],
                w2s.at[p, f], w2r.at[p, f], xdev(f),
            )
            for f in (1, 3, 2)
        ])
        wb[p][c, x] = wy[:, :, cols(o)]

    cu.wait()
    for cp in u1:
        cp.wait_recv()
    ro = lax.broadcasted_iota(jnp.int32, (256, 256), 0)
    ri = lax.broadcasted_iota(jnp.int32, (256, 256), 1)
    src = ((ro // 2) % 16) * 16 + (ro // 32) * 2 + ro % 2
    uperm[...] = jnp.dot(
        (src == ri).astype(BF), uprow[...].reshape(256, 128), preferred_element_type=F32
    ).astype(BF).reshape(NY, 32, 128)
    v1 = [
        remote(uperm.at[(y + d) % NY], upslab.at[y], v1s.at[d], v1r.at[d], ydev(d)) for d in SPREAD
    ]
    upslab[y] = uperm[y]

    def block_id(b, req):
        nxt = jnp.minimum(req + 1, start_s.shape[0] - 1)
        hit = jnp.where(start_s[nxt] <= b * 256, 1, 0)
        req = jnp.where(nxt > req, req + hit, req)
        ids[b] = home_s[adap_s[req]]
        return req

    lax.fori_loop(0, NY * ROW * BLK, block_id, jnp.int32(0))

    w3 = {}

    def w_forward(p):
        for cp in w2[p]:
            cp.wait_recv()
        w3[p] = remote(wb[p].at[c], wb[p].at[c], w3s.at[p], w3r.at[p], sib)

    def partial(p):
        w3[p].wait_recv()
        w = jnp.concatenate(
            [wb[p][k, j, i] for i in range(NY) for j in range(NX) for k in range(2)], axis=0
        )

        def rows(g, _):
            r = pl.ds(pl.multiple_of(g * 256, 256), 256)
            part[p, r, :] = jnp.dot(tok[r, :], w, preferred_element_type=F32)
            return 0

        lax.fori_loop(0, BLK, rows, 0)

    zc = {}

    def zsend(i, k, g):
        way = (1, -1)[i]
        zc[i, k, g] = remote(
            zs[i][k].at[g], zr[i][k].at[g], zss.at[i, k, g], zrs.at[i, k, g], tdev(way)
        )

    def zstep(i, k, p):
        for g in ((0, 1, 2, 3), (2, 3, 0, 1))[i]:
            if k == 0 and g // 2 != i:
                continue
            v = part[p, pl.ds(g * 256, 256), :]
            if (i, k - 1, g) in zc:
                zc[i, k - 1, g].wait_recv()
                v = v + zr[i][k - 1][g].astype(F32)
            zs[i][k][g] = v.astype(BF)
            zsend(i, k, g)

    ct.wait()
    w_forward(0)
    w_forward(1)
    partial(0)
    zstep(0, 0, 0)
    zstep(1, 0, 0)
    w_forward(2)
    partial(1)
    w_forward(3)
    partial(2)
    zstep(0, 1, 1)
    zstep(1, 1, 2)
    w_forward(4)
    partial(3)
    w_forward(5)
    partial(4)
    w_forward(6)
    w_forward(7)

    cs.wait()
    for cp in b1:
        cp.wait_recv()

    def pick(i, _):
        for j in range(ROW):
            for s in range(BLK):
                dsel[s][i, j] = slab[ids[i * (ROW * BLK) + (j * BLK + s)]]
        return 0

    lax.fori_loop(0, NY, pick, 0)
    b2 = []
    for s in range(BLK):
        b2.append([
            remote(
                dsel[s].at[(y + d) % NY], drow[s].at[y], b2s.at[s, d], b2r.at[s, d], ydev(d)
            )
            for d in SPREAD
        ])
        drow[s][y] = dsel[s][y]

    zstep(0, 2, 3)
    zstep(1, 2, 4)
    partial(5)
    partial(6)
    partial(7)
    zstep(0, 3, 5)
    zstep(1, 3, 6)

    for cp in v1:
        cp.wait_recv()
    half = lax.broadcasted_iota(jnp.int32, (16, 256), 0) // 2
    odd = lax.broadcasted_iota(jnp.int32, (16, 256), 0) % 2
    col = lax.broadcasted_iota(jnp.int32, (16, 256), 1)
    upall = upslab[...].reshape(256, 128)

    def pick_up(n, _):
        want = odd
        for k in range(8):
            want = jnp.where(half == k, want + 2 * ids[n * 8 + k], want)
        hot = (want == col).astype(BF)
        upsel[n] = jnp.dot(hot, upall, preferred_element_type=F32).astype(BF)
        return 0

    lax.fori_loop(0, 32, pick_up, 0)
    v2 = [
        remote(
            upsel.at[pl.ds(4 * ((y + d) % NY), 4)], uprcv.at[pl.ds(4 * y, 4)],
            v2s.at[d], v2r.at[d], ydev(d),
        )
        for d in SPREAD
    ]
    uprcv[pl.ds(4 * y, 4)] = upsel[pl.ds(4 * y, 4)]

    a2 = {}

    def row_send(s):
        for cp in b2[s]:
            cp.wait_recv()
        a2[s] = [
            remote(
                drow[s].at[:, (q + e) % ROW], dfin[s].at[q], a2s.at[s, e], a2r.at[s, e], rdev(e)
            )
            for e in SPREAD
        ]
        dfin[s][q] = drow[s][:, q]

    rs = {}

    def rank(s):
        for cp in a2[s]:
            cp.wait_recv()
        v = jnp.dot(
            tok[pl.ds(s * 256, 256), :], dfin[s][...].reshape(1024, 128), preferred_element_type=F32
        )
        rsend[s][...] = v.astype(BF).reshape(NT, 32, 128)
        rs[s] = [
            remote(rsend[s].at[(t + k) % NT], rrecv[s].at[t], rss.at[s, k], rsr.at[s, k], tdev(k))
            for k in SPREAD
        ]
        rrecv[s][t] = rsend[s][t]

    rg = {}

    def rank_sum(s):
        for cp in rs[s]:
            cp.wait_recv()
        v = jnp.sum(rrecv[s][...].astype(F32), axis=0)
        rfull[s][t] = v.astype(BF)
        rg[s] = [
            remote(rfull[s].at[t], rfull[s].at[t], rgs.at[s, k], rgr.at[s, k], tdev(k))
            for k in SPREAD
        ]

    row_send(0)
    row_send(1)
    rank(0)
    row_send(2)
    rank(1)
    rank_sum(0)
    row_send(3)

    for cp in v2:
        cp.wait_recv()
    ro = lax.broadcasted_iota(jnp.int32, (512, 512), 0)
    ri = lax.broadcasted_iota(jnp.int32, (512, 512), 1)
    src = ((ro // 2) % 8) * 64 + (ro // 64) * 8 + ((ro // 16) % 4) * 2 + ro % 2
    upx[...] = jnp.dot(
        (src == ri).astype(BF), uprcv[...].reshape(512, 128), preferred_element_type=F32
    ).astype(BF).reshape(ROW, BLK, 16, 128)
    u2 = [
        remote(upx.at[(q + e) % ROW], upg.at[q], u2s.at[e], u2r.at[e], rdev(e)) for e in SPREAD
    ]
    upg[q] = upx[q]

    rank(2)
    rank_sum(1)
    rank(3)
    rank_sum(2)
    rank_sum(3)

    for g in range(BLK):
        zc[0, 3, g].wait_recv()
        zc[1, 3, g].wait_recv()
        r = pl.ds(g * 256, 256)
        part[7, r, :] = part[7, r, :] + zr[0][3][g].astype(F32) + zr[1][3][g].astype(F32)
    for cp in u2:
        cp.wait_recv()
    for s in range(BLK):
        for cp in rg[s]:
            cp.wait_recv()
        delta = jnp.dot(
            rfull[s][...].reshape(256, 128), upg[:, s].reshape(128, 128), preferred_element_type=F32
        )
        r = pl.ds(s * 256, 256)
        out_ref[r, :] = (part[7, r, :] + ADAPTER_SCALE * delta).astype(BF)
    for cp in sent:
        cp.wait_send()


def body(tokens, value_weight, down, up, req_start, req_adapter, adapter_home):
    vm = pltpu.VMEM
    sem = pltpu.SemaphoreType.DMA
    any_ = pl.BlockSpec(memory_space=pl.ANY)
    smem = pl.BlockSpec(memory_space=pltpu.SMEM)
    return pl.pallas_call(
        kernel,
        out_shape=jax.ShapeDtypeStruct((1024, 128), BF),
        in_specs=[any_] * 4 + [smem] * 3,
        out_specs=pl.BlockSpec(memory_space=pltpu.VMEM),
        scratch_shapes=[
            vm((1024, 1024), BF),
            vm((NY, 16, 1024), BF),
            [vm((2, NX, NY, 16, 128), BF)] * NT,
            vm((16, NY, 16, 128), BF),
            vm((128, 16, 128), BF),
            [vm((NY, ROW, 16, 128), BF)] * BLK,
            [vm((NY, ROW, 16, 128), BF)] * BLK,
            [vm((ROW, NY, 16, 128), BF)] * BLK,
            vm((16, 16, 128), BF),
            vm((NY, 32, 128), BF),
            vm((NY, 32, 128), BF),
            vm((32, 16, 128), BF),
            vm((32, 16, 128), BF),
            vm((ROW, BLK, 16, 128), BF),
            vm((ROW, BLK, 16, 128), BF),
            [[vm((BLK, 256, 128), BF)] * 4] * 2,
            [[vm((BLK, 256, 128), BF)] * 4] * 2,
            vm((8, 1024, 128), F32),
            [vm((NT, 32, 128), BF)] * BLK,
            [vm((NT, 32, 128), BF)] * BLK,
            [vm((NT, 32, 128), BF)] * BLK,
            pltpu.SMEM((NY * ROW * BLK,), jnp.int32),
            sem((5,)),
            sem((8,)), sem((8,)), sem((8, 4)), sem((8, 4)), sem((8,)), sem((8,)),
            sem((8,)), sem((8,)), sem((8,)), sem((8,)), sem((8,)), sem((8,)), sem((8,)), sem((8,)),
            sem((4, 8)), sem((4, 8)), sem((8,)), sem((8,)), sem((4, 8)), sem((4, 8)), sem((8,)), sem((8,)),
            sem((2, 4, 4)), sem((2, 4, 4)),
            sem((4, 8)), sem((4, 8)), sem((4, 8)), sem((4, 8)),
        ],
        compiler_params=pltpu.CompilerParams(
            collective_id=0, has_side_effects=True, vmem_limit_bytes=60 * 1024 * 1024
        ),
    )(
        tokens, value_weight,
        down.reshape(2, ROW, NY, 16, 128), up.reshape(2, ROW, 16, 128),
        req_start, req_adapter, adapter_home,
    )


def solution(mesh):
    return jax.shard_map(
        body,
        mesh=mesh,
        in_specs=(
            P("ad", "tp"),
            P(("tp", "ad"), None),
            P("ad", "tp", None),
            P("ad", None, "tp"),
            P(),
            P(),
            P(),
        ),
        out_specs=P("ad", "tp"),
        check_vma=False,
    )
```

time: 216 us -> 91.2 us (0.42)
  waiting for transfers between devices: 99.4 us -> 0 us
  Pallas kernels: 0 us -> 88.9 us
  blocking collectives: 38 us -> 0 us
  starting transfers between devices: 32.6 us -> 0 us
  between operations: 14.2 us -> 0.01 us
  local copies, waits for them, and re-layouts: 15.4 us -> 1.67 us
  matrix products: 7.62 us -> 0 us
  other arithmetic: 7.53 us -> 0 us
    pallas_call x0 -> x1, Pallas kernels: none -> 88.9 us  [body(): pl.pallas_call(kernel, out_shape=jax.ShapeDtypeStruct((1024, 128), BF), i...]
    all_gather x1 -> x0, waiting for transfers between devices: 63.4 us -> none  [body(): lax.all_gather(value_weight, 'ad', axis=0, tiled=True)]
    psum x1 -> x0, blocking collectives: 38 us -> none  [body(): rank_full = lax.psum(rank_part, 'tp')]
    all_to_all x4 -> x0, waiting for transfers between devices: 35.2 us -> none  [the longest x1 26.6 us: body(): lax.all_to_all(down_out, 'ad', split_axis=1, concat_axis=1, tiled=True)]
    all_to_all x4 -> x0, starting transfers between devices: 32.6 us -> none  [the longest x1 10.6 us: body(): lax.all_to_all(up_send, 'ad', split_axis=1, concat_axis=0, tiled=True)]
    dot_general x3 -> x0, matrix products: 7.62 us -> none  [the longest x1 5.21 us: body(): jnp.dot(tokens, lax.all_gather(value_weight, 'ad', axis=0, tiled=True), p...]
    unnamed x7 -> x1, local copies, waits for them, and re-layouts: 6.62 us -> 1.67 us
    gather x4 -> x0, local copies, waits for them, and re-layouts: 4.93 us -> none  [the longest x1 1.76 us: body(): down_out = jnp.take(down_slab, fetch_rows, axis=0)]
  transfers between devices with their start and end apart: 6 -> 0, of which waited for: 4 -> 0; matrix products, arithmetic and copies ran while one was open for 13% -> 0% of each run, Pallas kernels for 0% -> 0%
where the time goes in v1:
time: 91.2 us; the launch traced here: 90.6 us
  Pallas kernels  88.9 us (97%)
  local copies, waits for them, and re-layouts  1.67 us (2%)
    pallas_call x1, Pallas kernels, body(): pl.pallas_call(kernel, out_shape=jax.ShapeDtypeStruct((1024, 128), BF), i...  88.9 us

profile of v1, /device:TPU:6, one launch (start us, length us, event | category | flops | bytes accessed | tf_op | source)
XLA Modules:
  0.0 90.6 jit_solution(3439794197399268888)
XLA Ops:
  0.0 88.9 %shard_map.73 = bf16[1024,128]{1,0:T(8,128)(2,1)} custom-call(bf16[1024,1024]{1,0:T(8,128)(2,1)} %tok_h.1, bf16[16,1024]{1,0:T(8,128)(2,1)} %vw_h.1, bf16[2,8,8,16,128]{4,3,2,1,0:T(8,128)(2,1)} %bitcast.2, bf16[2,8,16,128]{3,2,1,0:T(8,128)(2,1)} %bitcast.3, s32[64]{0:T(128)} %start_s.1, s32[64]{0:T(128)} %adap_s.1, s32[128]{0:T(128)} %home_s.1), custom_call_target="tpu_custom_call" | custom-call | tf_op jit(solution)/shard_map/pallas_call | solution.py:345
  88.9 1.7 %copy.9 = bf16[1024,128]{1,0:T(8,128)(2,1)} copy(bf16[1024,128]{1,0:T(8,128)(2,1)} %shard_map.73) | data formatting | bytes 524288

commit v2 on v1

--- a/solution.py
+++ b/solution.py
@@ -16,7 +16,7 @@
 NT = 8
 NY = 8
 BLK = 4
-SPREAD = (1, 7, 2, 6, 3, 5, 4)
+SPREAD = (4, 3, 5, 2, 6, 1, 7)
 PIECES = (4, 3, 5, 2, 6, 1, 7, 0)
 ADAPTER_SCALE = 2.0
 
@@ -26,7 +26,7 @@
     out_ref,
     tok, wy, wb, dnrow, slab, dsel, drow, dfin,
     uprow, uperm, upslab, upsel, uprcv, upx, upg,
-    zs, zr, part, rsend, rrecv, rfull, ids,
+    zs, zr, part, rsend, rrecv, rfull, order1, order2, ids,
     loc_sem, w1s, w1r, w2s, w2r, w3s, w3r,
     a1s, a1r, u1s, u1r, b1s, b1r, v1s, v1r,
     a2s, a2r, u2s, u2r, b2s, b2r, v2s, v2r,
@@ -60,6 +60,24 @@
         pl.semaphore_signal(bar, inc=1, device_id=rdev(e), device_id_type=MESH)
     for k in range(1, NT):
         pl.semaphore_signal(bar, inc=1, device_id=tdev(k), device_id_type=MESH)
+    ro = lax.broadcasted_iota(jnp.int32, (256, 256), 0)
+    ri = lax.broadcasted_iota(jnp.int32, (256, 256), 1)
+    src = ((ro // 2) % 16) * 16 + (ro // 32) * 2 + ro % 2
+    order1[...] = (src == ri).astype(BF)
+    ro = lax.broadcasted_iota(jnp.int32, (512, 512), 0)
+    ri = lax.broadcasted_iota(jnp.int32, (512, 512), 1)
+    src = ((ro // 2) % 8) * 64 + (ro // 64) * 8 + ((ro // 16) % 4) * 2 + ro % 2
+    order2[...] = (src == ri).astype(BF)
+
+    def block_id(b, req):
+        nxt = jnp.minimum(req + 1, start_s.shape[0] - 1)
+        hit = jnp.where(start_s[nxt] <= b * 256, 1, 0)
+        req = jnp.where(nxt > req, req + hit, req)
+        ids[b] = home_s[adap_s[req]]
+        return req
+
+    lax.fori_loop(0, NY * ROW * BLK, block_id, jnp.int32(0))
+
     pl.semaphore_wait(bar, 21)
 
     sent = []
@@ -119,25 +137,13 @@
     cu.wait()
     for cp in u1:
         cp.wait_recv()
-    ro = lax.broadcasted_iota(jnp.int32, (256, 256), 0)
-    ri = lax.broadcasted_iota(jnp.int32, (256, 256), 1)
-    src = ((ro // 2) % 16) * 16 + (ro // 32) * 2 + ro % 2
     uperm[...] = jnp.dot(
-        (src == ri).astype(BF), uprow[...].reshape(256, 128), preferred_element_type=F32
+        order1[...], uprow[...].reshape(256, 128), preferred_element_type=F32
     ).astype(BF).reshape(NY, 32, 128)
     v1 = [
         remote(uperm.at[(y + d) % NY], upslab.at[y], v1s.at[d], v1r.at[d], ydev(d)) for d in SPREAD
     ]
     upslab[y] = uperm[y]
-
-    def block_id(b, req):
-        nxt = jnp.minimum(req + 1, start_s.shape[0] - 1)
-        hit = jnp.where(start_s[nxt] <= b * 256, 1, 0)
-        req = jnp.where(nxt > req, req + hit, req)
-        ids[b] = home_s[adap_s[req]]
-        return req
-
-    lax.fori_loop(0, NY * ROW * BLK, block_id, jnp.int32(0))
 
     w3 = {}
 
@@ -201,15 +207,14 @@
     for cp in b1:
         cp.wait_recv()
 
-    def pick(i, _):
-        for j in range(ROW):
-            for s in range(BLK):
-                dsel[s][i, j] = slab[ids[i * (ROW * BLK) + (j * BLK + s)]]
-        return 0
-
-    lax.fori_loop(0, NY, pick, 0)
     b2 = []
     for s in range(BLK):
+        def pick(i, _):
+            for j in range(ROW):
+                dsel[s][i, j] = slab[ids[i * (ROW * BLK) + (j * BLK + s)]]
+            return 0
+
+        lax.fori_loop(0, NY, pick, 0)
         b2.append([
             remote(
                 dsel[s].at[(y + d) % NY], drow[s].at[y], b2s.at[s, d], b2r.at[s, d], ydev(d)
@@ -291,48 +296,48 @@
             for k in SPREAD
         ]
 
+    def out(s):
+        for cp in rg[s]:
+            cp.wait_recv()
+        delta = jnp.dot(
+            rfull[s][...].reshape(256, 128), upg[:, s].reshape(128, 128), preferred_element_type=F32
+        )
+        r = pl.ds(s * 256, 256)
+        out_ref[r, :] = (part[7, r, :] + ADAPTER_SCALE * delta).astype(BF)
+
     row_send(0)
     row_send(1)
     rank(0)
     row_send(2)
     rank(1)
     rank_sum(0)
-    row_send(3)
-
-    for cp in v2:
-        cp.wait_recv()
-    ro = lax.broadcasted_iota(jnp.int32, (512, 512), 0)
-    ri = lax.broadcasted_iota(jnp.int32, (512, 512), 1)
-    src = ((ro // 2) % 8) * 64 + (ro // 64) * 8 + ((ro // 16) % 4) * 2 + ro % 2
-    upx[...] = jnp.dot(
-        (src == ri).astype(BF), uprcv[...].reshape(512, 128), preferred_element_type=F32
-    ).astype(BF).reshape(ROW, BLK, 16, 128)
-    u2 = [
-        remote(upx.at[(q + e) % ROW], upg.at[q], u2s.at[e], u2r.at[e], rdev(e)) for e in SPREAD
-    ]
-    upg[q] = upx[q]
-
-    rank(2)
-    rank_sum(1)
-    rank(3)
-    rank_sum(2)
-    rank_sum(3)
-
     for g in range(BLK):
         zc[0, 3, g].wait_recv()
         zc[1, 3, g].wait_recv()
         r = pl.ds(g * 256, 256)
         part[7, r, :] = part[7, r, :] + zr[0][3][g].astype(F32) + zr[1][3][g].astype(F32)
+    row_send(3)
+    rank_sum(1)
+    rank(2)
+    for cp in v2:
+        cp.wait_recv()
+    upx[...] = jnp.dot(
+        order2[...], uprcv[...].reshape(512, 128), preferred_element_type=F32
+    ).astype(BF).reshape(ROW, BLK, 16, 128)
+    u2 = [
+        remote(upx.at[(q + e) % ROW], upg.at[q], u2s.at[e], u2r.at[e], rdev(e)) for e in SPREAD
+    ]
+    upg[q] = upx[q]
+
+    rank(3)
+    rank_sum(2)
     for cp in u2:
         cp.wait_recv()
-    for s in range(BLK):
-        for cp in rg[s]:
-            cp.wait_recv()
-        delta = jnp.dot(
-            rfull[s][...].reshape(256, 128), upg[:, s].reshape(128, 128), preferred_element_type=F32
-        )
-        r = pl.ds(s * 256, 256)
-        out_ref[r, :] = (part[7, r, :] + ADAPTER_SCALE * delta).astype(BF)
+    out(0)
+    out(1)
+    rank_sum(3)
+    out(2)
+    out(3)
     for cp in sent:
         cp.wait_send()
 
@@ -369,6 +374,8 @@
             [vm((NT, 32, 128), BF)] * BLK,
             [vm((NT, 32, 128), BF)] * BLK,
             [vm((NT, 32, 128), BF)] * BLK,
+            vm((256, 256), BF),
+            vm((512, 512), BF),
             pltpu.SMEM((NY * ROW * BLK,), jnp.int32),
             sem((5,)),
             sem((8,)), sem((8,)), sem((8, 4)), sem((8, 4)), sem((8,)), sem((8,)),

time: 91.2 us -> 87.1 us (0.955)
  Pallas kernels: 88.9 us -> 84 us
    pallas_call x1, Pallas kernels: 88.9 us -> 84 us  [body(): pl.pallas_call(kernel, out_shape=jax.ShapeDtypeStruct((1024, 128), BF), i...]
where the time goes in v2:
time: 87.1 us; the launch traced here: 85.7 us
  Pallas kernels  84 us (96%)
  local copies, waits for them, and re-layouts  1.67 us (2%)
    pallas_call x1, Pallas kernels, body(): pl.pallas_call(kernel, out_shape=jax.ShapeDtypeStruct((1024, 128), BF), i...  84 us

profile of v2, /device:TPU:6, one launch (start us, length us, event | category | flops | bytes accessed | tf_op | source)
XLA Modules:
  0.0 85.7 jit_solution(2665260106774765359)
XLA Ops:
  0.0 84.0 %shard_map.73 = bf16[1024,128]{1,0:T(8,128)(2,1)} custom-call(bf16[1024,1024]{1,0:T(8,128)(2,1)} %tok_h.1, bf16[16,1024]{1,0:T(8,128)(2,1)} %vw_h.1, bf16[2,8,8,16,128]{4,3,2,1,0:T(8,128)(2,1)} %bitcast.2, bf16[2,8,16,128]{3,2,1,0:T(8,128)(2,1)} %bitcast.3, s32[64]{0:T(128)} %start_s.1, s32[64]{0:T(128)} %adap_s.1, s32[128]{0:T(128)} %home_s.1), custom_call_target="tpu_custom_call" | custom-call | tf_op jit(solution)/shard_map/pallas_call | solution.py:350
  84.0 1.7 %copy.9 = bf16[1024,128]{1,0:T(8,128)(2,1)} copy(bf16[1024,128]{1,0:T(8,128)(2,1)} %shard_map.73) | data formatting | bytes 524288

commit v3 on v2

--- a/solution.py
+++ b/solution.py
@@ -174,10 +174,10 @@
         )
 
     def zstep(i, k, p):
-        for g in ((0, 1, 2, 3), (2, 3, 0, 1))[i]:
-            if k == 0 and g // 2 != i:
+        for g in ((0, 1), (1, 0))[i]:
+            if k == 0 and g != i:
                 continue
-            v = part[p, pl.ds(g * 256, 256), :]
+            v = part[p, pl.ds(g * 512, 512), :]
             if (i, k - 1, g) in zc:
                 zc[i, k - 1, g].wait_recv()
                 v = v + zr[i][k - 1][g].astype(F32)
@@ -311,10 +311,10 @@
     row_send(2)
     rank(1)
     rank_sum(0)
-    for g in range(BLK):
+    for g in range(2):
         zc[0, 3, g].wait_recv()
         zc[1, 3, g].wait_recv()
-        r = pl.ds(g * 256, 256)
+        r = pl.ds(g * 512, 512)
         part[7, r, :] = part[7, r, :] + zr[0][3][g].astype(F32) + zr[1][3][g].astype(F32)
     row_send(3)
     rank_sum(1)
@@ -368,8 +368,8 @@
             vm((32, 16, 128), BF),
             vm((ROW, BLK, 16, 128), BF),
             vm((ROW, BLK, 16, 128), BF),
-            [[vm((BLK, 256, 128), BF)] * 4] * 2,
-            [[vm((BLK, 256, 128), BF)] * 4] * 2,
+            [[vm((2, 512, 128), BF)] * 4] * 2,
+            [[vm((2, 512, 128), BF)] * 4] * 2,
             vm((8, 1024, 128), F32),
             [vm((NT, 32, 128), BF)] * BLK,
             [vm((NT, 32, 128), BF)] * BLK,
@@ -381,7 +381,7 @@
             sem((8,)), sem((8,)), sem((8, 4)), sem((8, 4)), sem((8,)), sem((8,)),
             sem((8,)), sem((8,)), sem((8,)), sem((8,)), sem((8,)), sem((8,)), sem((8,)), sem((8,)),
             sem((4, 8)), sem((4, 8)), sem((8,)), sem((8,)), sem((4, 8)), sem((4, 8)), sem((8,)), sem((8,)),
-            sem((2, 4, 4)), sem((2, 4, 4)),
+            sem((2, 4, 2)), sem((2, 4, 2)),
             sem((4, 8)), sem((4, 8)), sem((4, 8)), sem((4, 8)),
         ],
         compiler_params=pltpu.CompilerParams(

time: 87.1 us -> 86.7 us (level)
  no operation moved by 1% of the time
where the time goes in v3:
time: 86.7 us; the launch traced here: 85.3 us
  Pallas kernels  83.7 us (97%)
  local copies, waits for them, and re-layouts  1.67 us (2%)
    pallas_call x1, Pallas kernels, body(): pl.pallas_call(kernel, out_shape=jax.ShapeDtypeStruct((1024, 128), BF), i...  83.7 us

profile of v3, /device:TPU:6, one launch (start us, length us, event | category | flops | bytes accessed | tf_op | source)
XLA Modules:
  0.0 85.3 jit_solution(7657878202599943539)
XLA Ops:
  0.0 83.7 %shard_map.73 = bf16[1024,128]{1,0:T(8,128)(2,1)} custom-call(bf16[1024,1024]{1,0:T(8,128)(2,1)} %tok_h.1, bf16[16,1024]{1,0:T(8,128)(2,1)} %vw_h.1, bf16[2,8,8,16,128]{4,3,2,1,0:T(8,128)(2,1)} %bitcast.2, bf16[2,8,16,128]{3,2,1,0:T(8,128)(2,1)} %bitcast.3, s32[64]{0:T(128)} %start_s.1, s32[64]{0:T(128)} %adap_s.1, s32[128]{0:T(128)} %home_s.1), custom_call_target="tpu_custom_call" | custom-call | tf_op jit(solution)/shard_map/pallas_call | solution.py:350
  83.7 1.7 %copy.9 = bf16[1024,128]{1,0:T(8,128)(2,1)} copy(bf16[1024,128]{1,0:T(8,128)(2,1)} %shard_map.73) | data formatting | bytes 524288
